TPU v7x, 32 devices: a whole 2x2x4 slice. The times are simulated.
32 devices in a mesh: blk: 8 (over z, y), trk: 4 (over x, core).
Axes of the slice: x: 2, y: 2, z: 4, core: 2. Of those that a mesh axis runs over, the one named last changes fastest.
Arguments:
- row_block: int32 [8192, 1], P(('blk', 'trk')), may hold values from 0 to 7; in each aligned block of 256 rows (0 to 255, 256 to 511, ...) at most 64 rows name the same one
- row_hits: int32 [2, 8192], P(None, ('blk', 'trk')), may hold values from 0 to 63
- row_slot: int32 [8192], P(('blk', 'trk')), may hold values from 0 to 4
- track_kept: int32 [1024], P(('blk', 'trk')), may hold values 0 or 1
- row_derivs: bfloat16 [12, 8192], P(None, ('blk', 'trk')), may hold values from -0.75 to 0.75
- row_resid: bfloat16 [8192], P(('blk', 'trk')), may hold values from -6 to 6
- row_invsig: bfloat16 [8192], P(('blk', 'trk')), may hold values from 0.5 to 2
- pattern: int32 [8, 5], P('blk'), may hold values from 0 to 7, as said below
- prior: float32 [8, 384], P('blk'), may hold values from 0.2 to 3
Outputs:
- solution: float32 [8, 384], P('blk')
- gradient: float32 [8, 384], P('blk')
Inputs may be any that keep to these rules, and one draw needn't show every extreme that they name: `row_block`: among the rows of one device (aligned blocks of 256 rows) no block is named by more than 64 rows, and in every draw some device's rows name some block exactly 64 times. `pattern`: row k lists the blocks k - 2, k - 1, k, k + 1, k + 2 modulo 8, each once, in an order of its own.
All inputs are finite; a program needn't handle non-finite values. No bound on the sum of `track_kept` on one device may be relied on, other than what follows from the above.
Results may differ from a plain program's by a relative error of at most 0.0036.
The roundings to bfloat16 on the way count: a program that leaves them out, or rounds other values in their place, can miss the bound.
Values may be sent and summed in bfloat16 or wider, within the bound.
A program may use at most 64 MiB of HBM per device.

v0:
```python
import functools

import jax
import jax.numpy as jnp
from jax import lax
from jax.experimental import pallas as pl
from jax.experimental.pallas import tpu as pltpu
from jax.sharding import PartitionSpec as P

MODS = 64
PAR = 6
NB = 5
SEG = 8
ITERS = 2


epsilon = 1e-06


def passed_along(block, axis, distance):
    devices = range(lax.axis_size(axis))
    route = [((i - distance) % len(devices), i) for i in devices]
    return lax.ppermute(block, axis, route)


def project(initial_norm, diag_terms, off_terms, basis_list):
    size_count = len(diag_terms)
    zero_value = diag_terms[0] * 0.0
    rows_list = []
    for row_index in range(size_count + 1):
        entries = []
        for column in range(size_count):
            if row_index == column:
                entries.append(diag_terms[column])
            elif row_index == column + 1:
                entries.append(off_terms[column])
            elif column == row_index + 1:
                entries.append(off_terms[row_index])
            else:
                entries.append(zero_value)
        rows_list.append(jnp.stack(entries))
    tridiagonal = jnp.stack(rows_list)
    gram_matrix = jnp.dot(tridiagonal.T, tridiagonal, precision=lax.Precision.HIGHEST)
    target = initial_norm * tridiagonal[0]
    factor = jnp.linalg.cholesky(gram_matrix)
    forward = []
    for row_index in range(size_count):
        partial_sum = target[row_index]
        for column in range(row_index):
            partial_sum = partial_sum - factor[row_index, column] * forward[column]
        forward.append(partial_sum / factor[row_index, row_index])
    backward = [zero_value] * size_count
    for row_index in reversed(range(size_count)):
        partial_sum = forward[row_index]
        for column in range(row_index + 1, size_count):
            partial_sum = partial_sum - factor[column, row_index] * backward[column]
        backward[row_index] = partial_sum / factor[row_index, row_index]
    solution = backward[0] * basis_list[0]
    row_index = 1
    solution = solution + backward[row_index] * basis_list[row_index]
    return solution


def contract(left_rows, right_rows):
    return lax.dot_general(
        left_rows, right_rows, (((0,), (0,)), ((), ())), preferred_element_type=jnp.float32
    )


def on_device_large(
    row_block, row_hits, row_slot, track_kept, row_derivs, row_resid, row_invsig, pattern, prior
):
    row_count = row_resid.shape[0]
    owners = lax.axis_size("blk")
    capacity = 2 * row_count // owners
    order_size = MODS * PAR
    kept_rows = jnp.repeat(track_kept, SEG).astype(jnp.float32)
    scaling = kept_rows * row_invsig.astype(jnp.float32)
    scaled = (scaling[None, :] * row_derivs.astype(jnp.float32)).astype(jnp.bfloat16)
    weighted = (scaling * row_resid.astype(jnp.float32)).astype(jnp.bfloat16)
    destination = row_block[:, 0]
    member = (destination[:, None] == jnp.arange(owners, dtype=jnp.int32)[None, :]).astype(
        jnp.bfloat16
    )
    row_ids = jnp.arange(row_count, dtype=jnp.int32)
    earlier = (row_ids[:, None] > row_ids[None, :]).astype(jnp.bfloat16)
    before = jnp.dot(earlier, member, preferred_element_type=jnp.float32)
    rank_within = jnp.sum(before * member.astype(jnp.float32), axis=1).astype(jnp.int32)
    slot_place = destination * capacity + rank_within
    labels = jnp.stack([row_hits[0], row_hits[1], row_slot]).astype(jnp.bfloat16)
    record = jnp.concatenate([scaled, weighted[None, :], labels], axis=0)
    outgoing = (
        jnp.zeros((record.shape[0], owners * capacity), jnp.bfloat16).at[:, slot_place].set(record)
    )
    incoming = lax.all_to_all(outgoing, "blk", split_axis=1, concat_axis=1, tiled=True)
    column_ids = jnp.arange(order_size, dtype=jnp.int32)
    column_module = column_ids // PAR
    column_param = column_ids % PAR

    def expand(values, module_ids):
        spread = jnp.zeros((values.shape[1], order_size), jnp.bfloat16)
        for component in range(PAR):
            spread = jnp.where(
                column_param[None, :] == component, values[component][:, None], spread
            )
        return jnp.where(
            module_ids[:, None] == column_module[None, :], spread, jnp.zeros_like(spread)
        )

    first_module = incoming[2 * PAR + 1].astype(jnp.int32)
    second_module = incoming[2 * PAR + 2].astype(jnp.int32)
    slot_in = incoming[2 * PAR + 3].astype(jnp.int32)
    resid_in = incoming[2 * PAR]
    first_rows = expand(incoming[0:PAR], first_module)
    second_rows = expand(incoming[PAR : 2 * PAR], second_module)
    own_block = contract(first_rows, first_rows)
    grad_own = jnp.dot(resid_in, first_rows, preferred_element_type=jnp.float32)
    cross_list, partner_list, grad_list = ([], [], [])
    for slot_id in range(NB):
        masked = jnp.where((slot_in == slot_id)[:, None], second_rows, jnp.zeros_like(second_rows))
        cross_list.append(contract(first_rows, masked))
        partner_list.append(contract(masked, masked))
        grad_list.append(jnp.dot(resid_in, masked, preferred_element_type=jnp.float32))
    cross_blocks = jnp.stack(cross_list)
    partner_blocks = jnp.stack(partner_list)
    grad_partner = jnp.stack(grad_list)
    position = lax.axis_index("blk")
    neighbours = pattern[0]
    offset = (neighbours - position) % owners
    offset = jnp.where(offset > owners // 2, offset - owners, offset)

    def deliver(own_term, partner_terms):
        local_sum = own_term + jnp.sum(
            jnp.where((offset == 0)[:, None], partner_terms, 0.0), axis=0, keepdims=True
        )
        for shift_by in (-2, -1, 1, 2):
            sending = jnp.sum(
                jnp.where((offset == shift_by)[:, None], partner_terms, 0.0), axis=0, keepdims=True
            )
            local_sum = local_sum + passed_along(sending, "blk", shift_by)
        return lax.psum(local_sum, "trk")

    gradient = deliver(grad_own[None, :], grad_partner)
    initial_norm = jnp.sqrt(lax.psum(jnp.sum(gradient * gradient), "blk") + epsilon)
    current = gradient / initial_norm
    previous = jnp.zeros_like(gradient)
    beta_term = jnp.zeros((), jnp.float32)
    diag_terms, off_terms, basis_list = ([], [], [])
    for iteration in range(ITERS):
        result = jnp.where((offset == 0)[:, None], current, 0.0)
        for fetch_shift_by in (-2, -1, 1, 2):
            arrived = passed_along(current, "blk", -fetch_shift_by)
            result = result + jnp.where((offset == fetch_shift_by)[:, None], arrived, 0.0)
        operate_own_term = jnp.dot(own_block, current[0], precision=lax.Precision.HIGHEST)
        operate_own_term = operate_own_term + jnp.einsum(
            "kij,kj->i", cross_blocks, result, precision=lax.Precision.HIGHEST
        )
        operate_partner_terms = jnp.einsum(
            "kij,i->kj", cross_blocks, current[0], precision=lax.Precision.HIGHEST
        )
        operate_partner_terms = operate_partner_terms + jnp.einsum(
            "kij,kj->ki", partner_blocks, result, precision=lax.Precision.HIGHEST
        )
        image_vec = prior * current + deliver(operate_own_term[None, :], operate_partner_terms)
        alpha_term = lax.psum(jnp.sum(current * image_vec), "blk")
        direction = image_vec - alpha_term * current - beta_term * previous
        beta_next = jnp.sqrt(lax.psum(jnp.sum(direction * direction), "blk") + epsilon)
        diag_terms.append(alpha_term)
        off_terms.append(beta_next)
        basis_list.append(current)
        previous, current, beta_term = (current, direction / beta_next, beta_next)
    solution = project(initial_norm, diag_terms, off_terms, basis_list)
    return (solution, gradient)


LANES = 128
WIDE = 8
PHASES = ITERS + 1


def two_parts(value):
    high = value.astype(jnp.bfloat16)
    low = (value - high.astype(jnp.float32)).astype(jnp.bfloat16)
    return jnp.concatenate([high, low], axis=0)


def three_parts(value):
    high = value.astype(jnp.bfloat16).astype(jnp.float32)
    rest = value - high
    middle = rest.astype(jnp.bfloat16).astype(jnp.float32)
    return jnp.concatenate([high, middle, rest - middle], axis=0).astype(jnp.bfloat16)


def total(value):
    return jnp.sum(jnp.sum(value, axis=0, keepdims=True), axis=1, keepdims=True)


def kernel(
    owners,
    shares,
    block_ref,
    hits_ref,
    slot_ref,
    kept_ref,
    derivs_ref,
    resid_ref,
    invsig_ref,
    pattern_ref,
    prior_ref,
    out_ref,
    block_in,
    hits_in,
    slot_in,
    kept_in,
    derivs_in,
    resid_in,
    invsig_in,
    pattern_in,
    prior_in,
    input_sem,
    onehot,
    table,
    part,
    landed,
    blocks,
    full,
    table_send,
    table_recv,
    part_send,
    part_recv,
    block_send,
    block_recv,
    full_send,
    full_recv,
):
    blk, trk = lax.axis_index("blk"), lax.axis_index("trk")
    rows = block_ref.shape[1]
    tracks = kept_ref.shape[1]
    outside = (
        pattern_ref, kept_ref, invsig_ref, derivs_ref, resid_ref, block_ref, hits_ref, slot_ref, prior_ref
    )
    inside = (
        pattern_in, kept_in, invsig_in, derivs_in, resid_in, block_in, hits_in, slot_in, prior_in
    )
    fetches = [
        pltpu.make_async_copy(source, target, input_sem.at[i])
        for i, (source, target) in enumerate(zip(outside, inside))
    ]
    for one in fetches:
        one.start()
    modules = owners * MODS
    order_size = MODS * PAR
    per_share = LANES // MODS

    def other_blk(distance):
        return {"blk": lax.rem(blk + distance, owners), "trk": trk}

    pairs, width = shares // 2, shares // 2
    pair, half = trk // 2, lax.rem(trk, 2)
    sibling = {"blk": blk, "trk": pair * 2 + 1 - half}

    def other_pair(c, j):
        return {"blk": lax.rem(blk + c, owners), "trk": lax.rem(pair + j, pairs) * 2 + half}

    steps = [(c, j) for c in range(owners) for j in range(pairs) if c or j]
    steps.sort(key=lambda step: (abs(step[0] - owners // 2), -step[1]))
    peers = [sibling] + [other_pair(c, j) for c, j in steps]
    barrier = pltpu.get_barrier_semaphore()
    for peer in peers:
        pl.semaphore_signal(barrier, inc=1, device_id=peer, device_id_type=pl.DeviceIdType.MESH)

    def copy(source, target, send, recv, peer):
        return pltpu.make_async_remote_copy(
            src_ref=source,
            dst_ref=target,
            send_sem=send,
            recv_sem=recv,
            device_id=peer,
            device_id_type=pl.DeviceIdType.MESH,
        )

    started = []
    fetches[0].wait()

    table[blk, :, 0:NB] = pattern_in[...]
    pl.semaphore_wait(barrier, len(peers))
    sent = [
        copy(table.at[blk], table.at[blk], table_send.at[d - 1], table_recv.at[d - 1], other_blk(d))
        for d in range(1, owners)
    ]
    for one in sent:
        one.start()
    started += sent

    for one in fetches[1:]:
        one.wait()

    track_of = lax.broadcasted_iota(jnp.int32, (tracks, rows), 1) // SEG
    track_id = lax.broadcasted_iota(jnp.int32, (tracks, rows), 0)
    kept_rows = jnp.dot(
        jnp.broadcast_to(kept_in[...].astype(jnp.float32), (WIDE, tracks)).astype(jnp.bfloat16),
        (track_of == track_id).astype(jnp.float32).astype(jnp.bfloat16),
        preferred_element_type=jnp.float32,
    )[0:1]
    scaling = kept_rows * invsig_in[...].reshape(1, rows).astype(jnp.float32)
    scaled = (scaling * derivs_in[...].astype(jnp.float32)).astype(jnp.bfloat16).astype(jnp.float32)
    weighted = (scaling * resid_in[...].reshape(1, rows).astype(jnp.float32)).astype(jnp.bfloat16).astype(jnp.float32)
    none = jnp.zeros((WIDE - PAR, rows), jnp.float32)
    derivs = jnp.concatenate(
        [
            jnp.concatenate([scaled[0:PAR], none], axis=0),
            jnp.concatenate([scaled[PAR : 2 * PAR], none], axis=0),
        ],
        axis=1,
    )
    first_block = block_in[...]
    first_module = first_block * MODS + hits_in[0:1]
    module_ids = lax.broadcasted_iota(jnp.int32, (modules, rows), 0)
    onehot[:, 0:rows] = (module_ids == first_module).astype(jnp.float32).astype(jnp.bfloat16)

    place_row = lax.broadcasted_iota(jnp.int32, (order_size, LANES), 0) // PAR
    place_lane = lax.broadcasted_iota(jnp.int32, (order_size, LANES), 1)
    lane_half = lax.rem(blk, per_share)
    place = (place_lane == place_row + lane_half * MODS).astype(jnp.float32).astype(jnp.bfloat16)
    component = lax.broadcasted_iota(jnp.int32, (WIDE, order_size), 0)
    parameter = lax.broadcasted_iota(jnp.int32, (WIDE, order_size), 1)
    own_entry = component == lax.rem(parameter, PAR)
    spread_prior = jnp.where(own_entry, prior_in[...], 0.0)
    prior_parts = jnp.dot(three_parts(spread_prior), place, preferred_element_type=jnp.float32)
    own_prior = prior_parts[0:WIDE] + prior_parts[WIDE : 2 * WIDE] + prior_parts[2 * WIDE :]
    own_prior = jnp.where(trk == 0, own_prior, 0.0)
    own_share = blk // per_share
    prior = [jnp.where(own_share == j, own_prior, 0.0) for j in range(shares)]

    def in_order(vector):
        own = jnp.zeros((WIDE, LANES), jnp.float32)
        for j in range(shares):
            own = jnp.where(own_share == j, vector[:, j * LANES : (j + 1) * LANES], own)
        parts = three_parts(own)
        laid = lax.dot_general(
            parts, place, (((1,), (1,)), ((), ())), preferred_element_type=jnp.float32
        )
        laid = laid[0:WIDE] + laid[WIDE : 2 * WIDE] + laid[2 * WIDE :]
        return jnp.sum(jnp.where(own_entry, laid, 0.0), axis=0, keepdims=True)

    for one in sent:
        one.wait_recv()
    patterns = table[...].reshape(owners, LANES).astype(jnp.float32)
    block_ids = lax.broadcasted_iota(jnp.int32, (owners, rows), 0)
    names = (block_ids == first_block).astype(jnp.float32)
    slot = slot_in[...]
    second_block = jnp.zeros((1, rows), jnp.float32)
    for s in range(NB):
        value = jnp.sum(names * patterns[:, s : s + 1], axis=0, keepdims=True)
        second_block = jnp.where(slot == s, value, second_block)
    second_module = second_block.astype(jnp.int32) * MODS + hits_in[1:2]
    onehot[:, rows : 2 * rows] = (module_ids == second_module).astype(jnp.float32).astype(jnp.bfloat16)

    def scatter(row_values):
        both = jnp.concatenate([row_values, row_values], axis=1)
        summed = lax.dot_general(
            two_parts(derivs * both),
            onehot[...],
            (((1,), (1,)), ((), ())),
            preferred_element_type=jnp.float32,
        )
        return summed[0:WIDE] + summed[WIDE : 2 * WIDE]

    def gather(vector):
        read = jnp.dot(two_parts(vector), onehot[...], preferred_element_type=jnp.float32)
        read = read[0:WIDE] + read[WIDE : 2 * WIDE]
        along = jnp.sum(derivs * read, axis=0, keepdims=True)
        return along[:, 0:rows] + along[:, rows : 2 * rows]

    def add_up(phase, terms):
        for j in range(shares):
            part[phase, j // width, j % width] = terms[j]
        swap = copy(
            part.at[phase, 1 - half, :, 0:PAR],
            landed.at[phase, :, 0:PAR],
            part_send.at[phase],
            part_recv.at[phase],
            sibling,
        )
        swap.start()
        own = part[phase, half]
        swap.wait_recv()
        blocks[phase, blk, pair] = own + landed[phase]
        sent = [
            copy(
                blocks.at[phase, blk, pair, :, 0:PAR],
                blocks.at[phase, blk, pair, :, 0:PAR],
                block_send.at[phase, c, j],
                block_recv.at[phase, c, j],
                other_pair(c, j),
            )
            for c, j in steps
        ]
        for one in sent:
            one.start()
        for one in sent:
            one.wait_recv()
        summed = blocks[phase, 0, 0, :, 0:PAR]
        for k in range(1, owners * pairs):
            summed = summed + blocks[phase, k // pairs, k % pairs, :, 0:PAR]
        full[phase, half, :, 0:PAR] = summed
        join = copy(
            full.at[phase, half, :, 0:PAR],
            full.at[phase, half, :, 0:PAR],
            full_send.at[phase],
            full_recv.at[phase],
            sibling,
        )
        join.start()
        join.wait_recv()
        started.extend([swap, join] + sent)
        read = [full[phase, j // width, j % width, 0:PAR] for j in range(shares)]
        empty = jnp.zeros((WIDE - PAR, shares * LANES), jnp.float32)
        return jnp.concatenate([jnp.concatenate(read, axis=1), empty], axis=0)

    def pieces(vector):
        return [vector[:, j * LANES : (j + 1) * LANES] for j in range(shares)]

    gradient = add_up(0, pieces(scatter(weighted)))
    initial_norm = jnp.sqrt(total(gradient * gradient) + epsilon)
    current = gradient / initial_norm
    previous = jnp.zeros_like(gradient)
    beta_term = jnp.zeros((1, 1), jnp.float32)
    diag_terms, off_terms, basis_list = ([], [], [])
    for iteration in range(ITERS):
        terms = pieces(scatter(gather(current)))
        for j, values in enumerate(pieces(current)):
            terms[j] = terms[j] + prior[j] * values
        image_vec = add_up(iteration + 1, terms)
        alpha_term = total(current * image_vec)
        direction = image_vec - alpha_term * current - beta_term * previous
        beta_next = jnp.sqrt(total(direction * direction) + epsilon)
        diag_terms.append(alpha_term)
        off_terms.append(beta_next)
        basis_list.append(current)
        previous, current, beta_term = (current, direction / beta_next, beta_next)
    out_ref[1:2] = in_order(gradient)

    first, second = diag_terms
    below, last = off_terms
    corner = first * first + below * below
    side = first * below + below * second
    end = below * below + second * second + last * last
    root = jnp.sqrt(corner)
    lower = side / root
    tip = jnp.sqrt(end - lower * lower)
    forward = initial_norm * first / root
    forward_next = (initial_norm * below - lower * forward) / tip
    back_next = forward_next / tip
    back = (forward - lower * back_next) / root
    result = back * basis_list[0] + back_next * basis_list[1]
    out_ref[0:1] = in_order(result)
    for one in started:
        one.wait_send()


def on_device(
    row_block,
    row_hits,
    row_slot,
    track_kept,
    row_derivs,
    row_resid,
    row_invsig,
    pattern,
    prior,
    owners,
    shares,
):
    args = (
        row_block, row_hits, row_slot, track_kept, row_derivs, row_resid, row_invsig, pattern, prior
    )
    if owners * MODS != shares * LANES or shares % 2:
        return on_device_large(*args)
    rows = row_resid.shape[0]
    dma = pltpu.SemaphoreType.DMA
    tile = (WIDE, LANES)
    width = shares // 2
    out = pl.pallas_call(
        functools.partial(kernel, owners, shares),
        out_shape=jax.ShapeDtypeStruct((2, MODS * PAR), jnp.float32),
        in_specs=[pl.BlockSpec(memory_space=pltpu.HBM)] * 9,
        out_specs=pl.BlockSpec(memory_space=pltpu.VMEM),
        scratch_shapes=[
            pltpu.VMEM((1, rows), jnp.int32),
            pltpu.VMEM((2, rows), jnp.int32),
            pltpu.VMEM((1, rows), jnp.int32),
            pltpu.VMEM((1, track_kept.shape[0]), jnp.int32),
            pltpu.VMEM((2 * PAR, rows), jnp.bfloat16),
            pltpu.VMEM((rows,), jnp.bfloat16),
            pltpu.VMEM((rows,), jnp.bfloat16),
            pltpu.VMEM((1, NB), jnp.int32),
            pltpu.VMEM((1, MODS * PAR), jnp.float32),
            dma((9,)),
            pltpu.VMEM((owners * MODS, 2 * rows), jnp.bfloat16),
            pltpu.VMEM((owners, 1, LANES), jnp.int32),
            pltpu.VMEM((PHASES, 2, width) + tile, jnp.float32),
            pltpu.VMEM((PHASES, width) + tile, jnp.float32),
            pltpu.VMEM((PHASES, owners, shares // 2, width) + tile, jnp.float32),
            pltpu.VMEM((PHASES, 2, width) + tile, jnp.float32),
            dma((owners - 1,)),
            dma((owners - 1,)),
            dma((PHASES,)),
            dma((PHASES,)),
            dma((PHASES, owners, shares // 2)),
            dma((PHASES, owners, shares // 2)),
            dma((PHASES,)),
            dma((PHASES,)),
        ],
        compiler_params=pltpu.CompilerParams(
            collective_id=0, has_side_effects=True, vmem_limit_bytes=60 * 1024 * 1024
        ),
    )(
        row_block.reshape(1, rows),
        row_hits,
        row_slot.reshape(1, rows),
        track_kept.reshape(1, -1),
        row_derivs,
        row_resid,
        row_invsig,
        pattern,
        prior,
    )
    return out[0:1], out[1:2]


def solution(mesh):
    return jax.shard_map(
        functools.partial(on_device, owners=mesh.shape["blk"], shares=mesh.shape["trk"]),
        mesh=mesh,
        in_specs=(
            P(("blk", "trk"), None),
            P(None, ("blk", "trk")),
            P(("blk", "trk")),
            P(("blk", "trk")),
            P(None, ("blk", "trk")),
            P(("blk", "trk")),
            P(("blk", "trk")),
            P("blk", None),
            P("blk", None),
        ),
        out_specs=(P("blk", None), P("blk", None)),
        check_vma=False,
    )
```

profile of v0, /device:TPU:1, one launch (start us, length us, event | category | flops | bytes accessed | tf_op | source)
XLA Modules:
  0.0 36.5 jit_solution(17852012321872814622)
XLA Ops:
  0.6 34.5 %shard_map.104 = f32[2,384]{1,0:T(2,128)} custom-call(s32[1,256]{1,0:T(1,128)} %bitcast.3, s32[2,256]{1,0:T(2,128)} %hits_ref.1, s32[1,256]{1,0:T(1,128)} %bitcast.4, s32[1,32]{1,0:T(1,128)} %bitcast.5, bf16[12,256]{1,0:T(8,128)(2,1)} %derivs_ref.1, bf16[256]{0:T(256)(128)(2,1)} %resid_ref.1, bf16[256]{0:T(256)(128)(2,1)} %invsig_ref.1, s32[1,5]{1,0:T(1,128)} %pattern_ref.1, ...), custom_call_target="tpu_custom_call" | custom-call | tf_op jit(solution)/shard_map/pallas_call | solution.py:484
  35.2 1.3 %fusion = (f32[1,384]{1,0:T(1,128)}, f32[1,384]{1,0:T(1,128)}) fusion(f32[2,384]{1,0:T(2,128)} %shard_map.104), kind=kLoop, calls=%fused_computation | loop fusion | bytes 6144 | tf_op jit(solution)/shard_map/slice | solution.py:529
where the time goes:
time: 36.7 us; the launch traced here: 36.5 us
  Pallas kernels  34.5 us (94%)
  local copies, waits for them, and re-layouts  1.32 us (4%)
  between operations  0.64 us (2%)
    pallas_call x1, Pallas kernels, on_device(): pl.pallas_call(functools.partial(kernel, owners, shares), out_shape=jax.S...  34.5 us
    slice x1, local copies, waits for them, and re-layouts, on_device(): return (out[0:1], out[1:2])  1.32 us

commit v1 on v0

--- a/solution.py
+++ b/solution.py
@@ -176,12 +176,9 @@
 LANES = 128
 WIDE = 8
 PHASES = ITERS + 1
-
-
-def two_parts(value):
-    high = value.astype(jnp.bfloat16)
-    low = (value - high.astype(jnp.float32)).astype(jnp.bfloat16)
-    return jnp.concatenate([high, low], axis=0)
+RECORD = 16
+EXTRA = 3
+MESH = pl.DeviceIdType.MESH
 
 
 def three_parts(value):
@@ -191,8 +188,18 @@
     return jnp.concatenate([high, middle, rest - middle], axis=0).astype(jnp.bfloat16)
 
 
+def two_parts(value, axis):
+    high = value.astype(jnp.bfloat16)
+    low = (value - high.astype(jnp.float32)).astype(jnp.bfloat16)
+    return jnp.concatenate([high, low], axis=axis)
+
+
 def total(value):
     return jnp.sum(jnp.sum(value, axis=0, keepdims=True), axis=1, keepdims=True)
+
+
+def onehot(mask):
+    return mask.astype(jnp.float32).astype(jnp.bfloat16)
 
 
 def kernel(
@@ -218,29 +225,43 @@
     pattern_in,
     prior_in,
     input_sem,
-    onehot,
-    table,
-    part,
-    landed,
-    blocks,
-    full,
-    table_send,
-    table_recv,
-    part_send,
-    part_recv,
-    block_send,
-    block_recv,
-    full_send,
-    full_recv,
+    record,
+    extra,
+    spread,
+    labels,
+    grads,
+    mine,
+    other,
+    record_send,
+    record_recv,
+    extra_send,
+    extra_recv,
+    swap_send,
+    swap_recv,
 ):
     blk, trk = lax.axis_index("blk"), lax.axis_index("trk")
     rows = block_ref.shape[1]
     tracks = kept_ref.shape[1]
+    pairs = shares // 2
+    pair, half = trk // 2, lax.rem(trk, 2)
+    sibling = {"blk": blk, "trk": pair * 2 + 1 - half}
+    order_size = MODS * PAR
+    portion = order_size // shares
+
+    def peer(c, j):
+        return {"blk": lax.rem(blk + c, owners), "trk": lax.rem(pair + j, pairs) * 2 + half}
+
+    steps = [(c, j) for c in range(owners) for j in range(pairs) if c or j]
+    far_first = sorted(steps, key=lambda step: (abs(step[0] - owners // 2), -step[1]))
+    barrier = pltpu.get_barrier_semaphore()
+    for target in [peer(c, j) for c, j in far_first] + [sibling]:
+        pl.semaphore_signal(barrier, inc=1, device_id=target, device_id_type=MESH)
+
     outside = (
-        pattern_ref, kept_ref, invsig_ref, derivs_ref, resid_ref, block_ref, hits_ref, slot_ref, prior_ref
+        kept_ref, invsig_ref, derivs_ref, resid_ref, block_ref, hits_ref, slot_ref, prior_ref, pattern_ref
     )
     inside = (
-        pattern_in, kept_in, invsig_in, derivs_in, resid_in, block_in, hits_in, slot_in, prior_in
+        kept_in, invsig_in, derivs_in, resid_in, block_in, hits_in, slot_in, prior_in, pattern_in
     )
     fetches = [
         pltpu.make_async_copy(source, target, input_sem.at[i])
@@ -248,190 +269,145 @@
     ]
     for one in fetches:
         one.start()
-    modules = owners * MODS
-    order_size = MODS * PAR
-    per_share = LANES // MODS
-
-    def other_blk(distance):
-        return {"blk": lax.rem(blk + distance, owners), "trk": trk}
-
-    pairs, width = shares // 2, shares // 2
-    pair, half = trk // 2, lax.rem(trk, 2)
-    sibling = {"blk": blk, "trk": pair * 2 + 1 - half}
-
-    def other_pair(c, j):
-        return {"blk": lax.rem(blk + c, owners), "trk": lax.rem(pair + j, pairs) * 2 + half}
-
-    steps = [(c, j) for c in range(owners) for j in range(pairs) if c or j]
-    steps.sort(key=lambda step: (abs(step[0] - owners // 2), -step[1]))
-    peers = [sibling] + [other_pair(c, j) for c, j in steps]
-    barrier = pltpu.get_barrier_semaphore()
-    for peer in peers:
-        pl.semaphore_signal(barrier, inc=1, device_id=peer, device_id_type=pl.DeviceIdType.MESH)
-
-    def copy(source, target, send, recv, peer):
+    for one in fetches:
+        one.wait()
+
+    def copy(source, target, send, recv, device):
         return pltpu.make_async_remote_copy(
-            src_ref=source,
-            dst_ref=target,
-            send_sem=send,
-            recv_sem=recv,
-            device_id=peer,
-            device_id_type=pl.DeviceIdType.MESH,
-        )
-
-    started = []
-    fetches[0].wait()
-
-    table[blk, :, 0:NB] = pattern_in[...]
-    pl.semaphore_wait(barrier, len(peers))
-    sent = [
-        copy(table.at[blk], table.at[blk], table_send.at[d - 1], table_recv.at[d - 1], other_blk(d))
-        for d in range(1, owners)
-    ]
-    for one in sent:
-        one.start()
-    started += sent
-
-    for one in fetches[1:]:
-        one.wait()
+            src_ref=source, dst_ref=target, send_sem=send, recv_sem=recv, device_id=device, device_id_type=MESH
+        )
 
     track_of = lax.broadcasted_iota(jnp.int32, (tracks, rows), 1) // SEG
     track_id = lax.broadcasted_iota(jnp.int32, (tracks, rows), 0)
     kept_rows = jnp.dot(
-        jnp.broadcast_to(kept_in[...].astype(jnp.float32), (WIDE, tracks)).astype(jnp.bfloat16),
-        (track_of == track_id).astype(jnp.float32).astype(jnp.bfloat16),
+        onehot(jnp.broadcast_to(kept_in[...], (WIDE, tracks)) > 0),
+        onehot(track_of == track_id),
         preferred_element_type=jnp.float32,
     )[0:1]
     scaling = kept_rows * invsig_in[...].reshape(1, rows).astype(jnp.float32)
-    scaled = (scaling * derivs_in[...].astype(jnp.float32)).astype(jnp.bfloat16).astype(jnp.float32)
-    weighted = (scaling * resid_in[...].reshape(1, rows).astype(jnp.float32)).astype(jnp.bfloat16).astype(jnp.float32)
-    none = jnp.zeros((WIDE - PAR, rows), jnp.float32)
-    derivs = jnp.concatenate(
-        [
-            jnp.concatenate([scaled[0:PAR], none], axis=0),
-            jnp.concatenate([scaled[PAR : 2 * PAR], none], axis=0),
-        ],
-        axis=1,
-    )
-    first_block = block_in[...]
-    first_module = first_block * MODS + hits_in[0:1]
-    module_ids = lax.broadcasted_iota(jnp.int32, (modules, rows), 0)
-    onehot[:, 0:rows] = (module_ids == first_module).astype(jnp.float32).astype(jnp.bfloat16)
-
-    place_row = lax.broadcasted_iota(jnp.int32, (order_size, LANES), 0) // PAR
-    place_lane = lax.broadcasted_iota(jnp.int32, (order_size, LANES), 1)
-    lane_half = lax.rem(blk, per_share)
-    place = (place_lane == place_row + lane_half * MODS).astype(jnp.float32).astype(jnp.bfloat16)
-    component = lax.broadcasted_iota(jnp.int32, (WIDE, order_size), 0)
-    parameter = lax.broadcasted_iota(jnp.int32, (WIDE, order_size), 1)
-    own_entry = component == lax.rem(parameter, PAR)
-    spread_prior = jnp.where(own_entry, prior_in[...], 0.0)
-    prior_parts = jnp.dot(three_parts(spread_prior), place, preferred_element_type=jnp.float32)
-    own_prior = prior_parts[0:WIDE] + prior_parts[WIDE : 2 * WIDE] + prior_parts[2 * WIDE :]
-    own_prior = jnp.where(trk == 0, own_prior, 0.0)
-    own_share = blk // per_share
-    prior = [jnp.where(own_share == j, own_prior, 0.0) for j in range(shares)]
-
-    def in_order(vector):
-        own = jnp.zeros((WIDE, LANES), jnp.float32)
-        for j in range(shares):
-            own = jnp.where(own_share == j, vector[:, j * LANES : (j + 1) * LANES], own)
-        parts = three_parts(own)
-        laid = lax.dot_general(
-            parts, place, (((1,), (1,)), ((), ())), preferred_element_type=jnp.float32
-        )
-        laid = laid[0:WIDE] + laid[WIDE : 2 * WIDE] + laid[2 * WIDE :]
-        return jnp.sum(jnp.where(own_entry, laid, 0.0), axis=0, keepdims=True)
-
-    for one in sent:
-        one.wait_recv()
-    patterns = table[...].reshape(owners, LANES).astype(jnp.float32)
-    block_ids = lax.broadcasted_iota(jnp.int32, (owners, rows), 0)
-    names = (block_ids == first_block).astype(jnp.float32)
-    slot = slot_in[...]
-    second_block = jnp.zeros((1, rows), jnp.float32)
-    for s in range(NB):
-        value = jnp.sum(names * patterns[:, s : s + 1], axis=0, keepdims=True)
-        second_block = jnp.where(slot == s, value, second_block)
-    second_module = second_block.astype(jnp.int32) * MODS + hits_in[1:2]
-    onehot[:, rows : 2 * rows] = (module_ids == second_module).astype(jnp.float32).astype(jnp.bfloat16)
-
-    def scatter(row_values):
-        both = jnp.concatenate([row_values, row_values], axis=1)
-        summed = lax.dot_general(
-            two_parts(derivs * both),
-            onehot[...],
-            (((1,), (1,)), ((), ())),
-            preferred_element_type=jnp.float32,
-        )
-        return summed[0:WIDE] + summed[WIDE : 2 * WIDE]
-
-    def gather(vector):
-        read = jnp.dot(two_parts(vector), onehot[...], preferred_element_type=jnp.float32)
-        read = read[0:WIDE] + read[WIDE : 2 * WIDE]
-        along = jnp.sum(derivs * read, axis=0, keepdims=True)
-        return along[:, 0:rows] + along[:, rows : 2 * rows]
-
-    def add_up(phase, terms):
-        for j in range(shares):
-            part[phase, j // width, j % width] = terms[j]
-        swap = copy(
-            part.at[phase, 1 - half, :, 0:PAR],
-            landed.at[phase, :, 0:PAR],
-            part_send.at[phase],
-            part_recv.at[phase],
-            sibling,
-        )
+    scaled = scaling * derivs_in[...].astype(jnp.float32)
+    weighted = scaling * resid_in[...].reshape(1, rows).astype(jnp.float32)
+    record[blk, pair] = jnp.concatenate(
+        [scaled, weighted, hits_in[...].astype(jnp.float32), slot_in[...].astype(jnp.float32)], axis=0
+    ).astype(jnp.bfloat16)
+    block_row = block_in[...].astype(jnp.float32)
+    for piece in range(rows // LANES):
+        extra[blk, pair, piece : piece + 1] = block_row[:, piece * LANES : (piece + 1) * LANES]
+    last = rows // LANES
+    own = jnp.zeros((1, portion), jnp.float32)
+    for t in range(shares):
+        own = jnp.where(trk == t, prior_in[:, t * portion : (t + 1) * portion], own)
+    extra[blk, pair, last : last + 1, 0:portion] = own
+    extra[blk, pair, last : last + 1, portion : portion + NB] = pattern_in[...].astype(jnp.float32)
+
+    pl.semaphore_wait(barrier, len(steps) + 1)
+    extras = {
+        (c, j): copy(
+            extra.at[blk, pair], extra.at[blk, pair], extra_send.at[c, j], extra_recv.at[c, j], peer(c, j)
+        )
+        for c, j in far_first
+    }
+    records = {
+        (c, j): copy(
+            record.at[blk, pair], record.at[blk, pair], record_send.at[c, j], record_recv.at[c, j], peer(c, j)
+        )
+        for c, j in far_first
+    }
+    for step in far_first:
+        extras[step].start()
+    for step in far_first:
+        records[step].start()
+
+    block_ids = lax.broadcasted_iota(jnp.int32, (WIDE, rows), 0).astype(jnp.float32)
+    module_ids = lax.broadcasted_iota(jnp.int32, (MODS, 2 * rows), 0).astype(jnp.float32)
+    for step in far_first:
+        extras[step].wait_recv()
+    side = [extra[:, j, last, :] for j in range(pairs)]
+    columns = [
+        jnp.broadcast_to(side[0][:, portion + s : portion + s + 1], (WIDE, rows)) for s in range(NB)
+    ]
+
+    near_first = [(0, 0)] + far_first[::-1]
+    for c, j in near_first:
+        if c or j:
+            records[(c, j)].wait_recv()
+        b, p = lax.rem(blk + owners - c, owners), lax.rem(pair + pairs - j, pairs)
+        values = record[b, p].astype(jnp.float32)
+        first_block = jnp.concatenate([extra[b, p, i : i + 1] for i in range(last)], axis=1)
+        first = block_ids == first_block
+        slot = values[2 * PAR + 3 : 2 * PAR + 4]
+        coupled = columns[0]
+        for s in range(1, NB):
+            coupled = jnp.where(slot == s, columns[s], coupled)
+        second_block = jnp.sum(jnp.where(first, coupled, 0.0), axis=0, keepdims=True)
+        second = block_ids == second_block
+        terms = []
+        for i in range(PAR):
+            terms.append(
+                jnp.concatenate(
+                    [
+                        jnp.where(first, values[i : i + 1], 0.0),
+                        jnp.where(second, values[PAR + i : PAR + i + 1], 0.0),
+                    ],
+                    axis=1,
+                )
+            )
+        terms = jnp.concatenate(terms, axis=0)
+        spread[b, p] = terms
+        hits = jnp.concatenate(
+            [values[2 * PAR + 1 : 2 * PAR + 2], values[2 * PAR + 2 : 2 * PAR + 3]], axis=1
+        )
+        named = onehot(module_ids == hits)
+        labels[b, p, 0:MODS] = named
+        labels[b, p, MODS : 2 * MODS] = named
+        weight = values[2 * PAR : 2 * PAR + 1]
+        grads[b, p] = scatter(terms * jnp.concatenate([weight, weight], axis=1), named)
+
+    def add_up(phase, value):
+        mine[phase] = value
+        swap = copy(mine.at[phase], other.at[phase], swap_send.at[phase], swap_recv.at[phase], sibling)
         swap.start()
-        own = part[phase, half]
         swap.wait_recv()
-        blocks[phase, blk, pair] = own + landed[phase]
-        sent = [
-            copy(
-                blocks.at[phase, blk, pair, :, 0:PAR],
-                blocks.at[phase, blk, pair, :, 0:PAR],
-                block_send.at[phase, c, j],
-                block_recv.at[phase, c, j],
-                other_pair(c, j),
-            )
-            for c, j in steps
-        ]
-        for one in sent:
-            one.start()
-        for one in sent:
-            one.wait_recv()
-        summed = blocks[phase, 0, 0, :, 0:PAR]
-        for k in range(1, owners * pairs):
-            summed = summed + blocks[phase, k // pairs, k % pairs, :, 0:PAR]
-        full[phase, half, :, 0:PAR] = summed
-        join = copy(
-            full.at[phase, half, :, 0:PAR],
-            full.at[phase, half, :, 0:PAR],
-            full_send.at[phase],
-            full_recv.at[phase],
-            sibling,
-        )
-        join.start()
-        join.wait_recv()
-        started.extend([swap, join] + sent)
-        read = [full[phase, j // width, j % width, 0:PAR] for j in range(shares)]
-        empty = jnp.zeros((WIDE - PAR, shares * LANES), jnp.float32)
-        return jnp.concatenate([jnp.concatenate(read, axis=1), empty], axis=0)
-
-    def pieces(vector):
-        return [vector[:, j * LANES : (j + 1) * LANES] for j in range(shares)]
-
-    gradient = add_up(0, pieces(scatter(weighted)))
+        swaps.append(swap)
+        return value + other[phase]
+
+    swaps = []
+    gradient = grads[0, 0]
+    for k in range(1, owners * pairs):
+        gradient = gradient + grads[k // pairs, k % pairs]
+    gradient = add_up(0, gradient)
+
+    lane = lax.broadcasted_iota(jnp.int32, (LANES, order_size), 0)
+    column = lax.broadcasted_iota(jnp.int32, (LANES, order_size), 1)
+    prior = jnp.zeros((WIDE, order_size), jnp.float32)
+    for j in range(pairs):
+        module = lane // PAR + (2 * j + half) * (portion // PAR)
+        place = onehot(
+            (lane < portion) & (column == lax.rem(lane, PAR) * MODS + module)
+        )
+        laid = jnp.dot(three_parts(side[j]), place, preferred_element_type=jnp.float32)
+        prior = prior + (laid[0:WIDE] + laid[WIDE : 2 * WIDE] + laid[2 * WIDE :])
+    prior = jnp.concatenate([prior[:, i * MODS : (i + 1) * MODS] for i in range(PAR)], axis=0)
+
+    def matvec(vector):
+        parts = two_parts(vector, 1)
+        summed = jnp.zeros((PAR * WIDE, MODS), jnp.float32)
+        for k in range(owners * pairs):
+            b, p = k // pairs, k % pairs
+            terms = spread[b, p]
+            read = jnp.dot(parts, labels[b, p], preferred_element_type=jnp.float32)
+            along = jnp.sum(terms * read, axis=0, keepdims=True)
+            along = along[:, 0:rows] + along[:, rows : 2 * rows]
+            summed = summed + scatter(terms * jnp.concatenate([along, along], axis=1), labels[b, p, 0:MODS])
+        return summed + prior * vector
+
     initial_norm = jnp.sqrt(total(gradient * gradient) + epsilon)
     current = gradient / initial_norm
     previous = jnp.zeros_like(gradient)
     beta_term = jnp.zeros((1, 1), jnp.float32)
     diag_terms, off_terms, basis_list = ([], [], [])
     for iteration in range(ITERS):
-        terms = pieces(scatter(gather(current)))
-        for j, values in enumerate(pieces(current)):
-            terms[j] = terms[j] + prior[j] * values
-        image_vec = add_up(iteration + 1, terms)
+        image_vec = add_up(iteration + 1, matvec(current))
         alpha_term = total(current * image_vec)
         direction = image_vec - alpha_term * current - beta_term * previous
         beta_next = jnp.sqrt(total(direction * direction) + epsilon)
@@ -439,15 +415,34 @@
         off_terms.append(beta_next)
         basis_list.append(current)
         previous, current, beta_term = (current, direction / beta_next, beta_next)
+
+    module_row = lax.broadcasted_iota(jnp.int32, (MODS, order_size), 0)
+    module_of = lax.broadcasted_iota(jnp.int32, (MODS, order_size), 1) // PAR
+    place = onehot(module_row == module_of)
+    component = lax.broadcasted_iota(jnp.int32, (WIDE, order_size), 0)
+    parameter = lax.broadcasted_iota(jnp.int32, (WIDE, order_size), 1)
+    own_entry = component == lax.rem(parameter, PAR)
+    own_block = lax.broadcasted_iota(jnp.int32, (WIDE, MODS), 0) == blk
+
+    def in_order(vector):
+        own = [
+            jnp.sum(jnp.where(own_block, vector[i * WIDE : (i + 1) * WIDE], 0.0), axis=0, keepdims=True)
+            for i in range(PAR)
+        ]
+        own = jnp.concatenate(own + [jnp.zeros((WIDE - PAR, MODS), jnp.float32)], axis=0)
+        laid = jnp.dot(three_parts(own), place, preferred_element_type=jnp.float32)
+        laid = laid[0:WIDE] + laid[WIDE : 2 * WIDE] + laid[2 * WIDE :]
+        return jnp.sum(jnp.where(own_entry, laid, 0.0), axis=0, keepdims=True)
+
     out_ref[1:2] = in_order(gradient)
 
     first, second = diag_terms
-    below, last = off_terms
+    below, last_term = off_terms
     corner = first * first + below * below
-    side = first * below + below * second
-    end = below * below + second * second + last * last
+    side_term = first * below + below * second
+    end = below * below + second * second + last_term * last_term
     root = jnp.sqrt(corner)
-    lower = side / root
+    lower = side_term / root
     tip = jnp.sqrt(end - lower * lower)
     forward = initial_norm * first / root
     forward_next = (initial_norm * below - lower * forward) / tip
@@ -455,8 +450,15 @@
     back = (forward - lower * back_next) / root
     result = back * basis_list[0] + back_next * basis_list[1]
     out_ref[0:1] = in_order(result)
-    for one in started:
+    for one in list(extras.values()) + list(records.values()) + swaps:
         one.wait_send()
+
+
+def scatter(values, named):
+    summed = lax.dot_general(
+        two_parts(values, 0), named, (((1,), (1,)), ((), ())), preferred_element_type=jnp.float32
+    )
+    return summed[0 : PAR * WIDE] + summed[PAR * WIDE :]
 
 
 def on_device(
@@ -475,12 +477,12 @@
     args = (
         row_block, row_hits, row_slot, track_kept, row_derivs, row_resid, row_invsig, pattern, prior
     )
-    if owners * MODS != shares * LANES or shares % 2:
+    if owners != WIDE or shares % 2 or MODS % shares:
         return on_device_large(*args)
     rows = row_resid.shape[0]
     dma = pltpu.SemaphoreType.DMA
-    tile = (WIDE, LANES)
-    width = shares // 2
+    pairs = shares // 2
+    vector = (PAR * WIDE, MODS)
     out = pl.pallas_call(
         functools.partial(kernel, owners, shares),
         out_shape=jax.ShapeDtypeStruct((2, MODS * PAR), jnp.float32),
@@ -497,18 +499,17 @@
             pltpu.VMEM((1, NB), jnp.int32),
             pltpu.VMEM((1, MODS * PAR), jnp.float32),
             dma((9,)),
-            pltpu.VMEM((owners * MODS, 2 * rows), jnp.bfloat16),
-            pltpu.VMEM((owners, 1, LANES), jnp.int32),
-            pltpu.VMEM((PHASES, 2, width) + tile, jnp.float32),
-            pltpu.VMEM((PHASES, width) + tile, jnp.float32),
-            pltpu.VMEM((PHASES, owners, shares // 2, width) + tile, jnp.float32),
-            pltpu.VMEM((PHASES, 2, width) + tile, jnp.float32),
-            dma((owners - 1,)),
-            dma((owners - 1,)),
-            dma((PHASES,)),
-            dma((PHASES,)),
-            dma((PHASES, owners, shares // 2)),
-            dma((PHASES, owners, shares // 2)),
+            pltpu.VMEM((owners, pairs, RECORD, rows), jnp.bfloat16),
+            pltpu.VMEM((owners, pairs, EXTRA, LANES), jnp.float32),
+            pltpu.VMEM((owners, pairs, PAR * WIDE, 2 * rows), jnp.float32),
+            pltpu.VMEM((owners, pairs, 2 * MODS, 2 * rows), jnp.bfloat16),
+            pltpu.VMEM((owners, pairs) + vector, jnp.float32),
+            pltpu.VMEM((PHASES,) + vector, jnp.float32),
+            pltpu.VMEM((PHASES,) + vector, jnp.float32),
+            dma((owners, pairs)),
+            dma((owners, pairs)),
+            dma((owners, pairs)),
+            dma((owners, pairs)),
             dma((PHASES,)),
             dma((PHASES,)),
         ],

time: 36.7 us -> 26.1 us (0.71)
  Pallas kernels: 34.5 us -> 24 us
    pallas_call x1, Pallas kernels: 34.5 us -> 24 us  [on_device(): pl.pallas_call(functools.partial(kernel, owners, shares), out_shape=jax.S...]
where the time goes in v1:
time: 26.1 us; the launch traced here: 25.9 us
  Pallas kernels  24 us (92%)
  local copies, waits for them, and re-layouts  1.32 us (5%)
  between operations  0.64 us (2%)
    pallas_call x1, Pallas kernels, on_device(): pl.pallas_call(functools.partial(kernel, owners, shares), out_shape=jax.S...  24 us
    slice x1, local copies, waits for them, and re-layouts, on_device(): return (out[0:1], out[1:2])  1.32 us

profile of v1, /device:TPU:1, one launch (start us, length us, event | category | flops | bytes accessed | tf_op | source)
XLA Modules:
  0.0 25.9 jit_solution(12359061176786870020)
XLA Ops:
  0.6 24.0 %shard_map.104 = f32[2,384]{1,0:T(2,128)} custom-call(s32[1,256]{1,0:T(1,128)} %bitcast.3, s32[2,256]{1,0:T(2,128)} %hits_ref.1, s32[1,256]{1,0:T(1,128)} %bitcast.4, s32[1,32]{1,0:T(1,128)} %bitcast.5, bf16[12,256]{1,0:T(8,128)(2,1)} %derivs_ref.1, bf16[256]{0:T(256)(128)(2,1)} %resid_ref.1, bf16[256]{0:T(256)(128)(2,1)} %invsig_ref.1, s32[1,5]{1,0:T(1,128)} %pattern_ref.1, ...), custom_call_target="tpu_custom_call" | custom-call | tf_op jit(solution)/shard_map/pallas_call | solution.py:486
  24.6 1.3 %fusion = (f32[1,384]{1,0:T(1,128)}, f32[1,384]{1,0:T(1,128)}) fusion(f32[2,384]{1,0:T(2,128)} %shard_map.104), kind=kLoop, calls=%fused_computation | loop fusion | bytes 6144 | tf_op jit(solution)/shard_map/slice | solution.py:530

commit v2 on v1

--- a/solution.py
+++ b/solution.py
@@ -229,7 +229,8 @@
     extra,
     spread,
     labels,
-    grads,
+    turned,
+    products,
     mine,
     other,
     record_send,
@@ -318,7 +319,9 @@
     for step in far_first:
         records[step].start()
 
+    size = PAR * WIDE
     block_ids = lax.broadcasted_iota(jnp.int32, (WIDE, rows), 0).astype(jnp.float32)
+    lane_ids = lax.broadcasted_iota(jnp.int32, (rows, LANES), 1).astype(jnp.float32)
     module_ids = lax.broadcasted_iota(jnp.int32, (MODS, 2 * rows), 0).astype(jnp.float32)
     for step in far_first:
         extras[step].wait_recv()
@@ -327,11 +330,7 @@
         jnp.broadcast_to(side[0][:, portion + s : portion + s + 1], (WIDE, rows)) for s in range(NB)
     ]
 
-    near_first = [(0, 0)] + far_first[::-1]
-    for c, j in near_first:
-        if c or j:
-            records[(c, j)].wait_recv()
-        b, p = lax.rem(blk + owners - c, owners), lax.rem(pair + pairs - j, pairs)
+    def prepare(b, p):
         values = record[b, p].astype(jnp.float32)
         first_block = jnp.concatenate([extra[b, p, i : i + 1] for i in range(last)], axis=1)
         first = block_ids == first_block
@@ -354,28 +353,53 @@
             )
         terms = jnp.concatenate(terms, axis=0)
         spread[b, p] = terms
-        hits = jnp.concatenate(
-            [values[2 * PAR + 1 : 2 * PAR + 2], values[2 * PAR + 2 : 2 * PAR + 3]], axis=1
-        )
-        named = onehot(module_ids == hits)
+        upright = jnp.transpose(values)
+        upright = onehot(
+            jnp.concatenate(
+                [
+                    lane_ids == upright[:, 2 * PAR + 1 : 2 * PAR + 2],
+                    lane_ids == upright[:, 2 * PAR + 2 : 2 * PAR + 3],
+                ],
+                axis=0,
+            )
+        )
+        turned[b, p] = upright
+        weight = values[2 * PAR : 2 * PAR + 1]
+        halves = two_parts(terms * jnp.concatenate([weight, weight], axis=1), 0)
+        k = b * pairs + p
+        products[:, 2 * rows * k : 2 * rows * (k + 1)] = halves
+
+    for step in far_first[::-1]:
+        records[step].wait_recv()
+    for k in range(owners * pairs):
+        prepare(k // pairs, k % pairs)
+
+    swaps = []
+
+    def scattered():
+        upright = turned[...].reshape(owners * pairs * 2 * rows, LANES)
+        return joined(jnp.dot(products[...], upright, preferred_element_type=jnp.float32))
+
+    def exchange(phase, value, energy):
+        mine[phase, 0:size] = value
+        mine[phase, size:] = jnp.broadcast_to(energy, (WIDE, MODS))
+        swap = copy(mine.at[phase], other.at[phase], swap_send.at[phase], swap_recv.at[phase], sibling)
+        swap.start()
+        swaps.append(swap)
+
+    def received(phase):
+        swaps[phase].wait_recv()
+        both = mine[phase] + other[phase]
+        return both[0:size], both[size : size + 1, 0:1]
+
+    gradient = scattered()
+    exchange(0, gradient, jnp.zeros((1, 1), jnp.float32))
+    for k in range(owners * pairs):
+        b, p = k // pairs, k % pairs
+        hits = record[b, p, 2 * PAR + 1 : 2 * PAR + 3].astype(jnp.float32)
+        named = onehot(module_ids == jnp.concatenate([hits[0:1], hits[1:2]], axis=1))
         labels[b, p, 0:MODS] = named
         labels[b, p, MODS : 2 * MODS] = named
-        weight = values[2 * PAR : 2 * PAR + 1]
-        grads[b, p] = scatter(terms * jnp.concatenate([weight, weight], axis=1), named)
-
-    def add_up(phase, value):
-        mine[phase] = value
-        swap = copy(mine.at[phase], other.at[phase], swap_send.at[phase], swap_recv.at[phase], sibling)
-        swap.start()
-        swap.wait_recv()
-        swaps.append(swap)
-        return value + other[phase]
-
-    swaps = []
-    gradient = grads[0, 0]
-    for k in range(1, owners * pairs):
-        gradient = gradient + grads[k // pairs, k % pairs]
-    gradient = add_up(0, gradient)
 
     lane = lax.broadcasted_iota(jnp.int32, (LANES, order_size), 0)
     column = lax.broadcasted_iota(jnp.int32, (LANES, order_size), 1)
@@ -389,32 +413,22 @@
         prior = prior + (laid[0:WIDE] + laid[WIDE : 2 * WIDE] + laid[2 * WIDE :])
     prior = jnp.concatenate([prior[:, i * MODS : (i + 1) * MODS] for i in range(PAR)], axis=0)
 
-    def matvec(vector):
+    def apply(phase, vector):
         parts = two_parts(vector, 1)
-        summed = jnp.zeros((PAR * WIDE, MODS), jnp.float32)
+        energy = jnp.zeros((1, rows), jnp.float32)
         for k in range(owners * pairs):
             b, p = k // pairs, k % pairs
             terms = spread[b, p]
             read = jnp.dot(parts, labels[b, p], preferred_element_type=jnp.float32)
             along = jnp.sum(terms * read, axis=0, keepdims=True)
             along = along[:, 0:rows] + along[:, rows : 2 * rows]
-            summed = summed + scatter(terms * jnp.concatenate([along, along], axis=1), labels[b, p, 0:MODS])
-        return summed + prior * vector
-
-    initial_norm = jnp.sqrt(total(gradient * gradient) + epsilon)
-    current = gradient / initial_norm
-    previous = jnp.zeros_like(gradient)
-    beta_term = jnp.zeros((1, 1), jnp.float32)
-    diag_terms, off_terms, basis_list = ([], [], [])
-    for iteration in range(ITERS):
-        image_vec = add_up(iteration + 1, matvec(current))
-        alpha_term = total(current * image_vec)
-        direction = image_vec - alpha_term * current - beta_term * previous
-        beta_next = jnp.sqrt(total(direction * direction) + epsilon)
-        diag_terms.append(alpha_term)
-        off_terms.append(beta_next)
-        basis_list.append(current)
-        previous, current, beta_term = (current, direction / beta_next, beta_next)
+            energy = energy + along * along
+            products[:, 2 * rows * k : 2 * rows * (k + 1)] = two_parts(
+                terms * jnp.concatenate([along, along], axis=1), 0
+            )
+        summed = scattered()
+        damped = prior * vector
+        exchange(phase, summed + damped, total(energy) + total(damped * vector))
 
     module_row = lax.broadcasted_iota(jnp.int32, (MODS, order_size), 0)
     module_of = lax.broadcasted_iota(jnp.int32, (MODS, order_size), 1) // PAR
@@ -434,31 +448,34 @@
         laid = laid[0:WIDE] + laid[WIDE : 2 * WIDE] + laid[2 * WIDE :]
         return jnp.sum(jnp.where(own_entry, laid, 0.0), axis=0, keepdims=True)
 
-    out_ref[1:2] = in_order(gradient)
-
-    first, second = diag_terms
-    below, last_term = off_terms
-    corner = first * first + below * below
-    side_term = first * below + below * second
-    end = below * below + second * second + last_term * last_term
-    root = jnp.sqrt(corner)
-    lower = side_term / root
-    tip = jnp.sqrt(end - lower * lower)
-    forward = initial_norm * first / root
-    forward_next = (initial_norm * below - lower * forward) / tip
-    back_next = forward_next / tip
-    back = (forward - lower * back_next) / root
-    result = back * basis_list[0] + back_next * basis_list[1]
-    out_ref[0:1] = in_order(result)
+    gradient, _ = received(0)
+    apply(1, gradient)
+    norm = total(gradient * gradient) + epsilon
+    laid_gradient = in_order(gradient)
+    out_ref[1:2] = laid_gradient
+    image, energy = received(1)
+    first = energy / norm
+    direction = image - first * gradient
+    apply(2, direction)
+    scale = total(direction * direction) + epsilon * norm
+    below = scale / norm
+    laid_direction = in_order(direction)
+    image, energy = received(2)
+    second = energy / scale
+    rest = image - second * direction - below * gradient
+    end = total(rest * rest) / scale + epsilon
+    minor = first * second - below
+    determinant = minor * minor + end * (first * first + below)
+    out_ref[0:1] = (
+        (second * minor + first * end) / determinant * laid_gradient
+        - minor / determinant * laid_direction
+    )
     for one in list(extras.values()) + list(records.values()) + swaps:
         one.wait_send()
 
 
-def scatter(values, named):
-    summed = lax.dot_general(
-        two_parts(values, 0), named, (((1,), (1,)), ((), ())), preferred_element_type=jnp.float32
-    )
-    return summed[0 : PAR * WIDE] + summed[PAR * WIDE :]
+def joined(summed):
+    return summed[0 : PAR * WIDE, 0:MODS] + summed[PAR * WIDE :, 0:MODS]
 
 
 def on_device(
@@ -482,10 +499,9 @@
     rows = row_resid.shape[0]
     dma = pltpu.SemaphoreType.DMA
     pairs = shares // 2
-    vector = (PAR * WIDE, MODS)
     out = pl.pallas_call(
         functools.partial(kernel, owners, shares),
-        out_shape=jax.ShapeDtypeStruct((2, MODS * PAR), jnp.float32),
+        out_shape=pltpu.VMEM((2, MODS * PAR), jnp.float32),
         in_specs=[pl.BlockSpec(memory_space=pltpu.HBM)] * 9,
         out_specs=pl.BlockSpec(memory_space=pltpu.VMEM),
         scratch_shapes=[
@@ -503,9 +519,10 @@
             pltpu.VMEM((owners, pairs, EXTRA, LANES), jnp.float32),
             pltpu.VMEM((owners, pairs, PAR * WIDE, 2 * rows), jnp.float32),
             pltpu.VMEM((owners, pairs, 2 * MODS, 2 * rows), jnp.bfloat16),
-            pltpu.VMEM((owners, pairs) + vector, jnp.float32),
-            pltpu.VMEM((PHASES,) + vector, jnp.float32),
-            pltpu.VMEM((PHASES,) + vector, jnp.float32),
+            pltpu.VMEM((owners, pairs, 2 * rows, LANES), jnp.bfloat16),
+            pltpu.VMEM((2 * PAR * WIDE, owners * pairs * 2 * rows), jnp.bfloat16),
+            pltpu.VMEM((PHASES, PAR * WIDE + WIDE, MODS), jnp.float32),
+            pltpu.VMEM((PHASES, PAR * WIDE + WIDE, MODS), jnp.float32),
             dma((owners, pairs)),
             dma((owners, pairs)),
             dma((owners, pairs)),

time: 26.1 us -> 19.9 us (0.76)
  Pallas kernels: 24 us -> 18.5 us
  local copies, waits for them, and re-layouts: 1.32 us -> 0.57 us
    pallas_call x1, Pallas kernels: 24 us -> 18.5 us  [on_device(): pl.pallas_call(functools.partial(kernel, owners, shares), out_shape=pltpu...]
    slice x1, local copies, waits for them, and re-layouts: 1.32 us -> 0.57 us  [on_device(): return (out[0:1], out[1:2])]
where the time goes in v2:
time: 19.9 us; the launch traced here: 19.7 us
  Pallas kernels  18.5 us (93%)
  between operations  0.64 us (3%)
  local copies, waits for them, and re-layouts  0.57 us (3%)
    pallas_call x1, Pallas kernels, on_device(): pl.pallas_call(functools.partial(kernel, owners, shares), out_shape=pltpu...  18.5 us
    slice x1, local copies, waits for them, and re-layouts, on_device(): return (out[0:1], out[1:2])  0.57 us

profile of v2, /device:TPU:1, one launch (start us, length us, event | category | flops | bytes accessed | tf_op | source)
XLA Modules:
  0.0 19.7 jit_solution(15046449952171840813)
XLA Ops:
  0.6 18.5 %shard_map.104 = f32[2,384]{1,0:T(2,128)S(1)} custom-call(s32[1,256]{1,0:T(1,128)} %bitcast.3, s32[2,256]{1,0:T(2,128)} %hits_ref.1, s32[1,256]{1,0:T(1,128)} %bitcast.4, s32[1,32]{1,0:T(1,128)} %bitcast.5, bf16[12,256]{1,0:T(8,128)(2,1)} %derivs_ref.1, bf16[256]{0:T(256)(128)(2,1)} %resid_ref.1, bf16[256]{0:T(256)(128)(2,1)} %invsig_ref.1, ...), custom_call_target="tpu_custom_call" | custom-call | tf_op jit(solution)/shard_map/pallas_call | solution.py:502
  19.1 0.6 %fusion = (f32[1,384]{1,0:T(1,128)}, f32[1,384]{1,0:T(1,128)}) fusion(f32[2,384]{1,0:T(2,128)S(1)} %shard_map.104), kind=kLoop, calls=%fused_computation | loop fusion | bytes 6144 | tf_op jit(solution)/shard_map/slice | solution.py:547

commit v3 on v2

--- a/solution.py
+++ b/solution.py
@@ -249,13 +249,21 @@
     order_size = MODS * PAR
     portion = order_size // shares
 
-    def peer(c, j):
-        return {"blk": lax.rem(blk + c, owners), "trk": lax.rem(pair + j, pairs) * 2 + half}
-
-    steps = [(c, j) for c in range(owners) for j in range(pairs) if c or j]
-    far_first = sorted(steps, key=lambda step: (abs(step[0] - owners // 2), -step[1]))
+    me = blk * pairs + pair
+    line = owners * pairs
+    mirror = jnp.where(me < line // 2, 0, 1)
+    place = jnp.where(mirror == 1, line - 1 - me, me)
+    others = []
+    for n in reversed(range(line - 1)):
+        k = n + jnp.where(n >= place, 1, 0)
+        others.append(jnp.where(mirror == 1, line - 1 - k, k))
+
+    def peer(k):
+        return {"blk": k // pairs, "trk": lax.rem(k, pairs) * 2 + half}
+
+    peers = [peer(k) for k in others]
     barrier = pltpu.get_barrier_semaphore()
-    for target in [peer(c, j) for c, j in far_first] + [sibling]:
+    for target in peers + [sibling]:
         pl.semaphore_signal(barrier, inc=1, device_id=target, device_id_type=MESH)
 
     outside = (
@@ -301,30 +309,21 @@
     extra[blk, pair, last : last + 1, 0:portion] = own
     extra[blk, pair, last : last + 1, portion : portion + NB] = pattern_in[...].astype(jnp.float32)
 
-    pl.semaphore_wait(barrier, len(steps) + 1)
-    extras = {
-        (c, j): copy(
-            extra.at[blk, pair], extra.at[blk, pair], extra_send.at[c, j], extra_recv.at[c, j], peer(c, j)
-        )
-        for c, j in far_first
-    }
-    records = {
-        (c, j): copy(
-            record.at[blk, pair], record.at[blk, pair], record_send.at[c, j], record_recv.at[c, j], peer(c, j)
-        )
-        for c, j in far_first
-    }
-    for step in far_first:
-        extras[step].start()
-    for step in far_first:
-        records[step].start()
+    pl.semaphore_wait(barrier, len(peers) + 1)
+    sent, arriving = [], []
+    for k, target in zip(others, peers):
+        b, p = k // pairs, lax.rem(k, pairs)
+        for data, send, recv in ((extra, extra_send, extra_recv), (record, record_send, record_recv)):
+            sent.append(copy(data.at[blk, pair], data.at[blk, pair], send.at[b, p], recv.at[blk, pair], target))
+            arriving.append(copy(data.at[b, p], data.at[b, p], send.at[b, p], recv.at[b, p], target))
+    for one in sent:
+        one.start()
 
     size = PAR * WIDE
     block_ids = lax.broadcasted_iota(jnp.int32, (WIDE, rows), 0).astype(jnp.float32)
-    lane_ids = lax.broadcasted_iota(jnp.int32, (rows, LANES), 1).astype(jnp.float32)
     module_ids = lax.broadcasted_iota(jnp.int32, (MODS, 2 * rows), 0).astype(jnp.float32)
-    for step in far_first:
-        extras[step].wait_recv()
+    for one in arriving:
+        one.wait_recv()
     side = [extra[:, j, last, :] for j in range(pairs)]
     columns = [
         jnp.broadcast_to(side[0][:, portion + s : portion + s + 1], (WIDE, rows)) for s in range(NB)
@@ -353,31 +352,26 @@
             )
         terms = jnp.concatenate(terms, axis=0)
         spread[b, p] = terms
-        upright = jnp.transpose(values)
-        upright = onehot(
-            jnp.concatenate(
-                [
-                    lane_ids == upright[:, 2 * PAR + 1 : 2 * PAR + 2],
-                    lane_ids == upright[:, 2 * PAR + 2 : 2 * PAR + 3],
-                ],
-                axis=0,
-            )
-        )
+        hits = jnp.concatenate(
+            [values[2 * PAR + 1 : 2 * PAR + 2], values[2 * PAR + 2 : 2 * PAR + 3]], axis=1
+        )
+        named = onehot(module_ids == hits)
+        labels[b, p, 0:MODS] = named
+        labels[b, p, MODS : 2 * MODS] = named
+        upright = jnp.transpose(named)
         turned[b, p] = upright
         weight = values[2 * PAR : 2 * PAR + 1]
         halves = two_parts(terms * jnp.concatenate([weight, weight], axis=1), 0)
         k = b * pairs + p
         products[:, 2 * rows * k : 2 * rows * (k + 1)] = halves
 
-    for step in far_first[::-1]:
-        records[step].wait_recv()
     for k in range(owners * pairs):
         prepare(k // pairs, k % pairs)
 
     swaps = []
 
     def scattered():
-        upright = turned[...].reshape(owners * pairs * 2 * rows, LANES)
+        upright = turned[...].reshape(owners * pairs * 2 * rows, MODS)
         return joined(jnp.dot(products[...], upright, preferred_element_type=jnp.float32))
 
     def exchange(phase, value, energy):
@@ -394,12 +388,6 @@
 
     gradient = scattered()
     exchange(0, gradient, jnp.zeros((1, 1), jnp.float32))
-    for k in range(owners * pairs):
-        b, p = k // pairs, k % pairs
-        hits = record[b, p, 2 * PAR + 1 : 2 * PAR + 3].astype(jnp.float32)
-        named = onehot(module_ids == jnp.concatenate([hits[0:1], hits[1:2]], axis=1))
-        labels[b, p, 0:MODS] = named
-        labels[b, p, MODS : 2 * MODS] = named
 
     lane = lax.broadcasted_iota(jnp.int32, (LANES, order_size), 0)
     column = lax.broadcasted_iota(jnp.int32, (LANES, order_size), 1)
@@ -470,12 +458,12 @@
         (second * minor + first * end) / determinant * laid_gradient
         - minor / determinant * laid_direction
     )
-    for one in list(extras.values()) + list(records.values()) + swaps:
+    for one in sent + swaps:
         one.wait_send()
 
 
 def joined(summed):
-    return summed[0 : PAR * WIDE, 0:MODS] + summed[PAR * WIDE :, 0:MODS]
+    return summed[0 : PAR * WIDE] + summed[PAR * WIDE :]
 
 
 def on_device(
@@ -519,7 +507,7 @@
             pltpu.VMEM((owners, pairs, EXTRA, LANES), jnp.float32),
             pltpu.VMEM((owners, pairs, PAR * WIDE, 2 * rows), jnp.float32),
             pltpu.VMEM((owners, pairs, 2 * MODS, 2 * rows), jnp.bfloat16),
-            pltpu.VMEM((owners, pairs, 2 * rows, LANES), jnp.bfloat16),
+            pltpu.VMEM((owners, pairs, 2 * rows, MODS), jnp.bfloat16),
             pltpu.VMEM((2 * PAR * WIDE, owners * pairs * 2 * rows), jnp.bfloat16),
             pltpu.VMEM((PHASES, PAR * WIDE + WIDE, MODS), jnp.float32),
             pltpu.VMEM((PHASES, PAR * WIDE + WIDE, MODS), jnp.float32),

time: 19.9 us -> 18.6 us (0.935)
  Pallas kernels: 18.5 us -> 17.2 us
    pallas_call x1, Pallas kernels: 18.5 us -> 17.2 us  [on_device(): pl.pallas_call(functools.partial(kernel, owners, shares), out_shape=pltpu...]
where the time goes in v3:
time: 18.6 us; the launch traced here: 18.5 us
  Pallas kernels  17.2 us (92%)
  between operations  0.64 us (3%)
  local copies, waits for them, and re-layouts  0.57 us (3%)
    pallas_call x1, Pallas kernels, on_device(): pl.pallas_call(functools.partial(kernel, owners, shares), out_shape=pltpu...  17.2 us
    slice x1, local copies, waits for them, and re-layouts, on_device(): return (out[0:1], out[1:2])  0.57 us

profile of v3, /device:TPU:1, one launch (start us, length us, event | category | flops | bytes accessed | tf_op | source)
XLA Modules:
  0.0 18.5 jit_solution(1094849522204688066)
XLA Ops:
  0.6 17.2 %shard_map.104 = f32[2,384]{1,0:T(2,128)S(1)} custom-call(s32[1,256]{1,0:T(1,128)} %bitcast.3, s32[2,256]{1,0:T(2,128)} %hits_ref.1, s32[1,256]{1,0:T(1,128)} %bitcast.4, s32[1,32]{1,0:T(1,128)} %bitcast.5, bf16[12,256]{1,0:T(8,128)(2,1)} %derivs_ref.1, bf16[256]{0:T(256)(128)(2,1)} %resid_ref.1, bf16[256]{0:T(256)(128)(2,1)} %invsig_ref.1, ...), custom_call_target="tpu_custom_call" | custom-call | tf_op jit(solution)/shard_map/pallas_call | solution.py:490
  17.9 0.6 %fusion = (f32[1,384]{1,0:T(1,128)}, f32[1,384]{1,0:T(1,128)}) fusion(f32[2,384]{1,0:T(2,128)S(1)} %shard_map.104), kind=kLoop, calls=%fused_computation | loop fusion | bytes 6144 | tf_op jit(solution)/shard_map/slice | solution.py:535

commit v4 on v3

--- a/solution.py
+++ b/solution.py
@@ -321,7 +321,8 @@
 
     size = PAR * WIDE
     block_ids = lax.broadcasted_iota(jnp.int32, (WIDE, rows), 0).astype(jnp.float32)
-    module_ids = lax.broadcasted_iota(jnp.int32, (MODS, 2 * rows), 0).astype(jnp.float32)
+    module_ids = lax.broadcasted_iota(jnp.int32, (MODS, 2 * rows), 0).astype(jnp.float32).astype(jnp.bfloat16)
+    unit = jnp.ones((MODS, 2 * rows), jnp.bfloat16)
     for one in arriving:
         one.wait_recv()
     side = [extra[:, j, last, :] for j in range(pairs)]
@@ -352,27 +353,26 @@
             )
         terms = jnp.concatenate(terms, axis=0)
         spread[b, p] = terms
-        hits = jnp.concatenate(
-            [values[2 * PAR + 1 : 2 * PAR + 2], values[2 * PAR + 2 : 2 * PAR + 3]], axis=1
-        )
-        named = onehot(module_ids == hits)
+        labels_in = record[b, p, 2 * PAR : 2 * PAR + 3]
+        weight = jnp.concatenate([labels_in[0:1], labels_in[0:1]], axis=1)
+        hits = jnp.concatenate([labels_in[1:2], labels_in[2:3]], axis=1)
+        match = module_ids == hits
+        named = jnp.where(match, unit, jnp.zeros_like(unit))
+        heavy = jnp.where(match, jnp.broadcast_to(weight, match.shape), jnp.zeros_like(unit))
         labels[b, p, 0:MODS] = named
         labels[b, p, MODS : 2 * MODS] = named
-        upright = jnp.transpose(named)
-        turned[b, p] = upright
-        weight = values[2 * PAR : 2 * PAR + 1]
-        halves = two_parts(terms * jnp.concatenate([weight, weight], axis=1), 0)
+        turned[b, p] = jnp.transpose(jnp.concatenate([named, heavy], axis=0))
         k = b * pairs + p
-        products[:, 2 * rows * k : 2 * rows * (k + 1)] = halves
+        products[0:size, 2 * rows * k : 2 * rows * (k + 1)] = terms.astype(jnp.bfloat16)
 
     for k in range(owners * pairs):
         prepare(k // pairs, k % pairs)
 
     swaps = []
 
-    def scattered():
-        upright = turned[...].reshape(owners * pairs * 2 * rows, MODS)
-        return joined(jnp.dot(products[...], upright, preferred_element_type=jnp.float32))
+    def scattered(count):
+        upright = turned[...].reshape(owners * pairs * 2 * rows, LANES)
+        return jnp.dot(products[0:count], upright, preferred_element_type=jnp.float32)
 
     def exchange(phase, value, energy):
         mine[phase, 0:size] = value
@@ -386,7 +386,7 @@
         both = mine[phase] + other[phase]
         return both[0:size], both[size : size + 1, 0:1]
 
-    gradient = scattered()
+    gradient = scattered(size)[:, MODS:]
     exchange(0, gradient, jnp.zeros((1, 1), jnp.float32))
 
     lane = lax.broadcasted_iota(jnp.int32, (LANES, order_size), 0)
@@ -414,7 +414,8 @@
             products[:, 2 * rows * k : 2 * rows * (k + 1)] = two_parts(
                 terms * jnp.concatenate([along, along], axis=1), 0
             )
-        summed = scattered()
+        summed = scattered(2 * size)
+        summed = summed[0:size, 0:MODS] + summed[size:, 0:MODS]
         damped = prior * vector
         exchange(phase, summed + damped, total(energy) + total(damped * vector))
 
@@ -462,10 +463,6 @@
         one.wait_send()
 
 
-def joined(summed):
-    return summed[0 : PAR * WIDE] + summed[PAR * WIDE :]
-
-
 def on_device(
     row_block,
     row_hits,
@@ -482,7 +479,7 @@
     args = (
         row_block, row_hits, row_slot, track_kept, row_derivs, row_resid, row_invsig, pattern, prior
     )
-    if owners != WIDE or shares % 2 or MODS % shares:
+    if owners != WIDE or 2 * MODS != LANES or shares % 2 or MODS % shares:
         return on_device_large(*args)
     rows = row_resid.shape[0]
     dma = pltpu.SemaphoreType.DMA
@@ -507,7 +504,7 @@
             pltpu.VMEM((owners, pairs, EXTRA, LANES), jnp.float32),
             pltpu.VMEM((owners, pairs, PAR * WIDE, 2 * rows), jnp.float32),
             pltpu.VMEM((owners, pairs, 2 * MODS, 2 * rows), jnp.bfloat16),
-            pltpu.VMEM((owners, pairs, 2 * rows, MODS), jnp.bfloat16),
+            pltpu.VMEM((owners, pairs, 2 * rows, LANES), jnp.bfloat16),
             pltpu.VMEM((2 * PAR * WIDE, owners * pairs * 2 * rows), jnp.bfloat16),
             pltpu.VMEM((PHASES, PAR * WIDE + WIDE, MODS), jnp.float32),
             pltpu.VMEM((PHASES, PAR * WIDE + WIDE, MODS), jnp.float32),

time: 18.6 us -> 18.3 us (0.984)
  Pallas kernels: 17.2 us -> 16.9 us
    pallas_call x1, Pallas kernels: 17.2 us -> 16.9 us  [on_device(): pl.pallas_call(functools.partial(kernel, owners, shares), out_shape=pltpu...]
where the time goes in v4:
time: 18.3 us; the launch traced here: 18.1 us
  Pallas kernels  16.9 us (92%)
  between operations  0.64 us (3%)
  local copies, waits for them, and re-layouts  0.57 us (3%)
    pallas_call x1, Pallas kernels, on_device(): pl.pallas_call(functools.partial(kernel, owners, shares), out_shape=pltpu...  16.9 us
    slice x1, local copies, waits for them, and re-layouts, on_device(): return (out[0:1], out[1:2])  0.57 us

profile of v4, /device:TPU:1, one launch (start us, length us, event | category | flops | bytes accessed | tf_op | source)
XLA Modules:
  0.0 18.1 jit_solution(10362350921959693478)
XLA Ops:
  0.6 16.9 %shard_map.104 = f32[2,384]{1,0:T(2,128)S(1)} custom-call(s32[1,256]{1,0:T(1,128)} %bitcast.3, s32[2,256]{1,0:T(2,128)} %hits_ref.1, s32[1,256]{1,0:T(1,128)} %bitcast.4, s32[1,32]{1,0:T(1,128)} %bitcast.5, bf16[12,256]{1,0:T(8,128)(2,1)} %derivs_ref.1, bf16[256]{0:T(256)(128)(2,1)} %resid_ref.1, bf16[256]{0:T(256)(128)(2,1)} %invsig_ref.1, ...), custom_call_target="tpu_custom_call" | custom-call | tf_op jit(solution)/shard_map/pallas_call | solution.py:487
  17.5 0.6 %fusion = (f32[1,384]{1,0:T(1,128)}, f32[1,384]{1,0:T(1,128)}) fusion(f32[2,384]{1,0:T(2,128)S(1)} %shard_map.104), kind=kLoop, calls=%fused_computation | loop fusion | bytes 6144 | tf_op jit(solution)/shard_map/slice | solution.py:532

commit v5 on v4

--- a/solution.py
+++ b/solution.py
@@ -296,26 +296,25 @@
     scaling = kept_rows * invsig_in[...].reshape(1, rows).astype(jnp.float32)
     scaled = scaling * derivs_in[...].astype(jnp.float32)
     weighted = scaling * resid_in[...].reshape(1, rows).astype(jnp.float32)
-    record[blk, pair] = jnp.concatenate(
+    record[me] = jnp.concatenate(
         [scaled, weighted, hits_in[...].astype(jnp.float32), slot_in[...].astype(jnp.float32)], axis=0
     ).astype(jnp.bfloat16)
     block_row = block_in[...].astype(jnp.float32)
     for piece in range(rows // LANES):
-        extra[blk, pair, piece : piece + 1] = block_row[:, piece * LANES : (piece + 1) * LANES]
+        extra[me, piece : piece + 1] = block_row[:, piece * LANES : (piece + 1) * LANES]
     last = rows // LANES
     own = jnp.zeros((1, portion), jnp.float32)
     for t in range(shares):
         own = jnp.where(trk == t, prior_in[:, t * portion : (t + 1) * portion], own)
-    extra[blk, pair, last : last + 1, 0:portion] = own
-    extra[blk, pair, last : last + 1, portion : portion + NB] = pattern_in[...].astype(jnp.float32)
+    extra[me, last : last + 1, 0:portion] = own
+    extra[me, last : last + 1, portion : portion + NB] = pattern_in[...].astype(jnp.float32)
 
     pl.semaphore_wait(barrier, len(peers) + 1)
-    sent, arriving = [], []
+    sent = []
     for k, target in zip(others, peers):
         b, p = k // pairs, lax.rem(k, pairs)
         for data, send, recv in ((extra, extra_send, extra_recv), (record, record_send, record_recv)):
-            sent.append(copy(data.at[blk, pair], data.at[blk, pair], send.at[b, p], recv.at[blk, pair], target))
-            arriving.append(copy(data.at[b, p], data.at[b, p], send.at[b, p], recv.at[b, p], target))
+            sent.append(copy(data.at[me], data.at[me], send.at[b, p], recv.at[0], target))
     for one in sent:
         one.start()
 
@@ -323,16 +322,19 @@
     block_ids = lax.broadcasted_iota(jnp.int32, (WIDE, rows), 0).astype(jnp.float32)
     module_ids = lax.broadcasted_iota(jnp.int32, (MODS, 2 * rows), 0).astype(jnp.float32).astype(jnp.bfloat16)
     unit = jnp.ones((MODS, 2 * rows), jnp.bfloat16)
-    for one in arriving:
-        one.wait_recv()
-    side = [extra[:, j, last, :] for j in range(pairs)]
+    rest_of = pl.ds(0, len(peers))
+    for data, send, recv in ((extra, extra_send, extra_recv), (record, record_send, record_recv)):
+        copy(data.at[rest_of], data.at[rest_of], send.at[0, 0], recv.at[0], sibling).wait_recv()
+    side = [
+        jnp.concatenate([extra[b * pairs + j, last : last + 1] for b in range(owners)], axis=0) for j in range(pairs)
+    ]
     columns = [
         jnp.broadcast_to(side[0][:, portion + s : portion + s + 1], (WIDE, rows)) for s in range(NB)
     ]
 
     def prepare(b, p):
-        values = record[b, p].astype(jnp.float32)
-        first_block = jnp.concatenate([extra[b, p, i : i + 1] for i in range(last)], axis=1)
+        values = record[b * pairs + p].astype(jnp.float32)
+        first_block = jnp.concatenate([extra[b * pairs + p, i : i + 1] for i in range(last)], axis=1)
         first = block_ids == first_block
         slot = values[2 * PAR + 3 : 2 * PAR + 4]
         coupled = columns[0]
@@ -353,7 +355,7 @@
             )
         terms = jnp.concatenate(terms, axis=0)
         spread[b, p] = terms
-        labels_in = record[b, p, 2 * PAR : 2 * PAR + 3]
+        labels_in = record[b * pairs + p, 2 * PAR : 2 * PAR + 3]
         weight = jnp.concatenate([labels_in[0:1], labels_in[0:1]], axis=1)
         hits = jnp.concatenate([labels_in[1:2], labels_in[2:3]], axis=1)
         match = module_ids == hits
@@ -437,11 +439,14 @@
         laid = laid[0:WIDE] + laid[WIDE : 2 * WIDE] + laid[2 * WIDE :]
         return jnp.sum(jnp.where(own_entry, laid, 0.0), axis=0, keepdims=True)
 
+    for one in sent:
+        one.wait_send()
     gradient, _ = received(0)
     apply(1, gradient)
     norm = total(gradient * gradient) + epsilon
     laid_gradient = in_order(gradient)
     out_ref[1:2] = laid_gradient
+    swaps[0].wait_send()
     image, energy = received(1)
     first = energy / norm
     direction = image - first * gradient
@@ -449,6 +454,7 @@
     scale = total(direction * direction) + epsilon * norm
     below = scale / norm
     laid_direction = in_order(direction)
+    swaps[1].wait_send()
     image, energy = received(2)
     second = energy / scale
     rest = image - second * direction - below * gradient
@@ -459,8 +465,7 @@
         (second * minor + first * end) / determinant * laid_gradient
         - minor / determinant * laid_direction
     )
-    for one in sent + swaps:
-        one.wait_send()
+    swaps[-1].wait_send()
 
 
 def on_device(
@@ -500,8 +505,8 @@
             pltpu.VMEM((1, NB), jnp.int32),
             pltpu.VMEM((1, MODS * PAR), jnp.float32),
             dma((9,)),
-            pltpu.VMEM((owners, pairs, RECORD, rows), jnp.bfloat16),
-            pltpu.VMEM((owners, pairs, EXTRA, LANES), jnp.float32),
+            pltpu.VMEM((owners * pairs, RECORD, rows), jnp.bfloat16),
+            pltpu.VMEM((owners * pairs, EXTRA, LANES), jnp.float32),
             pltpu.VMEM((owners, pairs, PAR * WIDE, 2 * rows), jnp.float32),
             pltpu.VMEM((owners, pairs, 2 * MODS, 2 * rows), jnp.bfloat16),
             pltpu.VMEM((owners, pairs, 2 * rows, LANES), jnp.bfloat16),
@@ -509,9 +514,9 @@
             pltpu.VMEM((PHASES, PAR * WIDE + WIDE, MODS), jnp.float32),
             pltpu.VMEM((PHASES, PAR * WIDE + WIDE, MODS), jnp.float32),
             dma((owners, pairs)),
+            dma((1,)),
             dma((owners, pairs)),
-            dma((owners, pairs)),
-            dma((owners, pairs)),
+            dma((1,)),
             dma((PHASES,)),
             dma((PHASES,)),
         ],

time: 18.3 us -> 17.9 us (0.978)
  Pallas kernels: 16.9 us -> 16.5 us
    pallas_call x1, Pallas kernels: 16.9 us -> 16.5 us  [on_device(): pl.pallas_call(functools.partial(kernel, owners, shares), out_shape=pltpu...]
where the time goes in v5:
time: 17.9 us; the launch traced here: 17.7 us
  Pallas kernels  16.5 us (92%)
  between operations  0.64 us (4%)
  local copies, waits for them, and re-layouts  0.57 us (3%)
    pallas_call x1, Pallas kernels, on_device(): pl.pallas_call(functools.partial(kernel, owners, shares), out_shape=pltpu...  16.5 us
    slice x1, local copies, waits for them, and re-layouts, on_device(): return (out[0:1], out[1:2])  0.57 us

profile of v5, /device:TPU:1, one launch (start us, length us, event | category | flops | bytes accessed | tf_op | source)
XLA Modules:
  0.0 17.7 jit_solution(1460534637515604501)
XLA Ops:
  0.6 16.5 %shard_map.104 = f32[2,384]{1,0:T(2,128)S(1)} custom-call(s32[1,256]{1,0:T(1,128)} %bitcast.3, s32[2,256]{1,0:T(2,128)} %hits_ref.1, s32[1,256]{1,0:T(1,128)} %bitcast.4, s32[1,32]{1,0:T(1,128)} %bitcast.5, bf16[12,256]{1,0:T(8,128)(2,1)} %derivs_ref.1, bf16[256]{0:T(256)(128)(2,1)} %resid_ref.1, bf16[256]{0:T(256)(128)(2,1)} %invsig_ref.1, ...), custom_call_target="tpu_custom_call" | custom-call | tf_op jit(solution)/shard_map/pallas_call | solution.py:492
  17.1 0.6 %fusion = (f32[1,384]{1,0:T(1,128)}, f32[1,384]{1,0:T(1,128)}) fusion(f32[2,384]{1,0:T(2,128)S(1)} %shard_map.104), kind=kLoop, calls=%fused_computation | loop fusion | bytes 6144 | tf_op jit(solution)/shard_map/slice | solution.py:537

commit v6 on v5

--- a/solution.py
+++ b/solution.py
@@ -444,26 +444,30 @@
     gradient, _ = received(0)
     apply(1, gradient)
     norm = total(gradient * gradient) + epsilon
+    per_norm = 1.0 / norm
     laid_gradient = in_order(gradient)
     out_ref[1:2] = laid_gradient
     swaps[0].wait_send()
     image, energy = received(1)
-    first = energy / norm
+    first = energy * per_norm
     direction = image - first * gradient
     apply(2, direction)
     scale = total(direction * direction) + epsilon * norm
-    below = scale / norm
+    per_scale = 1.0 / scale
+    below = scale * per_norm
+    corner = first * first + below
+    beyond = below * gradient
     laid_direction = in_order(direction)
     swaps[1].wait_send()
     image, energy = received(2)
-    second = energy / scale
-    rest = image - second * direction - below * gradient
-    end = total(rest * rest) / scale + epsilon
+    second = energy * per_scale
+    rest = (image - beyond) - second * direction
+    end = total(rest * rest) * per_scale + epsilon
     minor = first * second - below
-    determinant = minor * minor + end * (first * first + below)
+    per_determinant = 1.0 / (minor * minor + end * corner)
     out_ref[0:1] = (
-        (second * minor + first * end) / determinant * laid_gradient
-        - minor / determinant * laid_direction
+        ((second * minor + first * end) * per_determinant) * laid_gradient
+        - (minor * per_determinant) * laid_direction
     )
     swaps[-1].wait_send()
 

time: 17.9 us -> 17.9 us (level)
  no operation moved by 1% of the time
where the time goes in v6:
time: 17.9 us; the launch traced here: 17.7 us
  Pallas kernels  16.5 us (92%)
  between operations  0.64 us (4%)
  local copies, waits for them, and re-layouts  0.57 us (3%)
    pallas_call x1, Pallas kernels, on_device(): pl.pallas_call(functools.partial(kernel, owners, shares), out_shape=pltpu...  16.5 us
    slice x1, local copies, waits for them, and re-layouts, on_device(): return (out[0:1], out[1:2])  0.57 us

profile of v6, /device:TPU:1, one launch (start us, length us, event | category | flops | bytes accessed | tf_op | source)
XLA Modules:
  0.0 17.7 jit_solution(14239905691204726830)
XLA Ops:
  0.6 16.5 %shard_map.104 = f32[2,384]{1,0:T(2,128)S(1)} custom-call(s32[1,256]{1,0:T(1,128)} %bitcast.3, s32[2,256]{1,0:T(2,128)} %hits_ref.1, s32[1,256]{1,0:T(1,128)} %bitcast.4, s32[1,32]{1,0:T(1,128)} %bitcast.5, bf16[12,256]{1,0:T(8,128)(2,1)} %derivs_ref.1, bf16[256]{0:T(256)(128)(2,1)} %resid_ref.1, bf16[256]{0:T(256)(128)(2,1)} %invsig_ref.1, ...), custom_call_target="tpu_custom_call" | custom-call | tf_op jit(solution)/shard_map/pallas_call | solution.py:496
  17.1 0.6 %fusion = (f32[1,384]{1,0:T(1,128)}, f32[1,384]{1,0:T(1,128)}) fusion(f32[2,384]{1,0:T(2,128)S(1)} %shard_map.104), kind=kLoop, calls=%fused_computation | loop fusion | bytes 6144 | tf_op jit(solution)/shard_map/slice | solution.py:541

commit v7 on v6

--- a/solution.py
+++ b/solution.py
@@ -406,6 +406,8 @@
     def apply(phase, vector):
         parts = two_parts(vector, 1)
         energy = jnp.zeros((1, rows), jnp.float32)
+        summed = jnp.zeros((2 * size, LANES), jnp.float32)
+        chunk = owners * pairs // 2
         for k in range(owners * pairs):
             b, p = k // pairs, k % pairs
             terms = spread[b, p]
@@ -416,7 +418,12 @@
             products[:, 2 * rows * k : 2 * rows * (k + 1)] = two_parts(
                 terms * jnp.concatenate([along, along], axis=1), 0
             )
-        summed = scattered(2 * size)
+            if k % chunk == chunk - 1:
+                begin = k + 1 - chunk
+                upright = turned[begin // pairs : (k + 1) // pairs].reshape(chunk * 2 * rows, LANES)
+                summed = summed + jnp.dot(
+                    products[:, 2 * rows * begin : 2 * rows * (k + 1)], upright, preferred_element_type=jnp.float32
+                )
         summed = summed[0:size, 0:MODS] + summed[size:, 0:MODS]
         damped = prior * vector
         exchange(phase, summed + damped, total(energy) + total(damped * vector))

time: 17.9 us -> 17.9 us (level)
  no operation moved by 1% of the time
where the time goes in v7:
time: 17.9 us; the launch traced here: 17.7 us
  Pallas kernels  16.5 us (92%)
  between operations  0.64 us (4%)
  local copies, waits for them, and re-layouts  0.57 us (3%)
    pallas_call x1, Pallas kernels, on_device(): pl.pallas_call(functools.partial(kernel, owners, shares), out_shape=pltpu...  16.5 us
    slice x1, local copies, waits for them, and re-layouts, on_device(): return (out[0:1], out[1:2])  0.57 us

profile of v7, /device:TPU:1, one launch (start us, length us, event | category | flops | bytes accessed | tf_op | source)
XLA Modules:
  0.0 17.7 jit_solution(12435580173729349339)
XLA Ops:
  0.6 16.5 %shard_map.104 = f32[2,384]{1,0:T(2,128)S(1)} custom-call(s32[1,256]{1,0:T(1,128)} %bitcast.3, s32[2,256]{1,0:T(2,128)} %hits_ref.1, s32[1,256]{1,0:T(1,128)} %bitcast.4, s32[1,32]{1,0:T(1,128)} %bitcast.5, bf16[12,256]{1,0:T(8,128)(2,1)} %derivs_ref.1, bf16[256]{0:T(256)(128)(2,1)} %resid_ref.1, bf16[256]{0:T(256)(128)(2,1)} %invsig_ref.1, ...), custom_call_target="tpu_custom_call" | custom-call | tf_op jit(solution)/shard_map/pallas_call | solution.py:503
  17.2 0.6 %fusion = (f32[1,384]{1,0:T(1,128)}, f32[1,384]{1,0:T(1,128)}) fusion(f32[2,384]{1,0:T(2,128)S(1)} %shard_map.104), kind=kLoop, calls=%fused_computation | loop fusion | bytes 6144 | tf_op jit(solution)/shard_map/slice | solution.py:548
